TPU v7x, 32 devices: a whole 2x2x4 slice. The times are simulated.
32 devices in a mesh: group: 2 (over y), row: 8 (over z, core), chan: 2 (over x).
Axes of the slice: x: 2, y: 2, z: 4, core: 2. Of those that a mesh axis runs over, the one named last changes fastest.
Arguments:
- pair: bfloat16 [1024, 512, 128], P(('group', 'row'), 'chan'), parts along dimension 0, may hold values from -6 to 6
- token_mask: int32 [1024], P('group'), parts along dimension 0, may hold values 0 or 1
- band_start: int32 [2], P('group'), parts along dimension 0, may hold values from 0 to 496
- w_left: bfloat16 [128, 64], replicated, may hold values from -0.5 to 0.5
- w_left_gate: bfloat16 [128, 64], replicated, may hold values from -0.5 to 0.5
- w_right: bfloat16 [128, 64], replicated, may hold values from -0.5 to 0.5
- w_right_gate: bfloat16 [128, 64], replicated, may hold values from -0.5 to 0.5
- w_gate_out: bfloat16 [128, 128], replicated, may hold values from -0.5 to 0.5
- w_out: bfloat16 [64, 128], replicated, may hold values from -0.75 to 0.75
- norm_in_gain: float32 [128], replicated, may hold values from 0.1 to 1.9
- norm_out_gain: float32 [64], replicated, may hold values from 0.1 to 1.9
Outputs:
- band_update: bfloat16 [32, 512, 128], P(('group', 'row'), 'chan'), parts along dimension 0
There are 2 independent parts, one for each index of `group`. A program takes and returns all parts, laid end to end along the dimension named above; an argument that names none is the same for every part. Nothing has to cross between parts.
Inputs may be any that keep to these rules, and one draw needn't show every extreme that they name: `band_start`: the band of 16 rows lies inside the map.
All inputs are finite; a program needn't handle non-finite values.
Results may differ from a plain program's by a relative error of at most 0.0087.
Values may be sent and summed in bfloat16 or wider, within the bound.
A program may use at most 128 MiB of HBM per device.

v0:
```python
import jax
import jax.numpy as jnp
from jax import lax
from jax.sharding import PartitionSpec as P

BAND_DEV = 2


def from_behind(shard, axis, by):
    size = lax.axis_size(axis)
    return lax.ppermute(shard, axis, [(i, (i + by) % size) for i in range(size)])


def layer_norm(values, gain):
    values = values.astype(jnp.float32)
    middle = jnp.mean(values, -1, keepdims=True)
    spread = jnp.mean(jnp.square(values - middle), -1, keepdims=True)
    return (values - middle) * lax.rsqrt(spread + 1e-05) * gain


def channel_gated(normed, w_value, w_gate):
    value = jnp.einsum("rkd,dc->crk", normed, w_value, preferred_element_type=jnp.float32)
    opener = jnp.einsum("rkd,dc->crk", normed, w_gate, preferred_element_type=jnp.float32)
    return jax.nn.sigmoid(opener) * value


def body(
    pair,
    token_mask,
    band_start,
    w_left,
    w_left_gate,
    w_right,
    w_right_gate,
    w_gate_out,
    w_out,
    norm_in_gain,
    norm_out_gain,
):
    rows_dev, cols_dev, width = pair.shape
    cycles = lax.axis_size("row")
    place = lax.axis_index("row")
    lane = lax.axis_index("chan")
    band = BAND_DEV * cycles
    valid = token_mask.astype(jnp.float32)
    row_valid = lax.dynamic_slice_in_dim(valid, place * rows_dev, rows_dev)
    col_valid = lax.dynamic_slice_in_dim(valid, lane * cols_dev, cols_dev)
    normed = layer_norm(pair, norm_in_gain).astype(jnp.bfloat16)
    right = (
        channel_gated(normed, w_right, w_right_gate)
        * row_valid[None, :, None]
        * col_valid[None, None, :]
    ).astype(jnp.bfloat16)
    start = band_start[0]
    offsets = start + jnp.arange(band, dtype=jnp.int32) - place * rows_dev
    inside = ((offsets >= 0) & (offsets < rows_dev)).astype(jnp.float32)
    clipped = jnp.clip(offsets, 0, rows_dev - 1)
    raw_rows = jnp.take(pair, clipped, axis=0).astype(jnp.float32) * inside[:, None, None]
    own_rows = lax.psum_scatter(
        raw_rows.astype(jnp.bfloat16), "row", scatter_dimension=0, tiled=True
    )
    own_normed = layer_norm(own_rows, norm_in_gain).astype(jnp.bfloat16)
    own_valid = lax.dynamic_slice_in_dim(valid, start + place * BAND_DEV, BAND_DEV)
    left_slot = (
        channel_gated(own_normed, w_left, w_left_gate)
        * own_valid[None, :, None]
        * col_valid[None, None, :]
    ).astype(jnp.bfloat16)
    own_opener = jnp.einsum(
        "ikd,de->eik", own_normed, w_gate_out, preferred_element_type=jnp.float32
    )
    gate_slot = jax.nn.sigmoid(own_opener).astype(jnp.bfloat16)
    left_cols = lax.all_to_all(left_slot, "chan", split_axis=0, concat_axis=2, tiled=True)
    right_cols = lax.all_to_all(right, "chan", split_axis=0, concat_axis=2, tiled=True)

    def block_product(block):
        return jnp.einsum("cik,cjk->cij", block, right_cols, preferred_element_type=jnp.float32)

    empty = jnp.zeros((right_cols.shape[0], band, rows_dev), jnp.float32)
    first = lax.dynamic_update_slice_in_dim(empty, block_product(left_cols), place * BAND_DEV, 1)

    def advance(step, carry):
        block, total = carry
        block = from_behind(block, "row", 1)
        slot = (place - step) % cycles
        total = lax.dynamic_update_slice_in_dim(total, block_product(block), slot * BAND_DEV, 1)
        return (block, total)

    held, summed = lax.fori_loop(1, cycles, advance, (left_cols, first))
    product = summed.astype(jnp.bfloat16)
    returned = lax.all_to_all(
        lax.all_to_all(product, "row", split_axis=1, concat_axis=2, tiled=True),
        "chan",
        split_axis=2,
        concat_axis=0,
        tiled=True,
    )
    product_tile = jnp.transpose(returned, (1, 2, 0))
    product_normed = layer_norm(product_tile, norm_out_gain).astype(jnp.bfloat16)
    projected = jnp.dot(product_normed, w_out, preferred_element_type=jnp.float32)
    gate_tile = jnp.transpose(gate_slot, (1, 2, 0)).astype(jnp.float32)
    return (projected * gate_tile).astype(jnp.bfloat16)


def solution(mesh):
    return jax.shard_map(
        body,
        mesh=mesh,
        in_specs=(
            P(("group", "row"), "chan", None),
            P("group"),
            P("group"),
            P(),
            P(),
            P(),
            P(),
            P(),
            P(),
            P(),
            P(),
        ),
        out_specs=P(("group", "row"), "chan", None),
        check_vma=False,
    )
```

profile of v0, /device:TPU:0, one launch (start us, length us, event | category | flops | bytes accessed | tf_op | source)
XLA Modules:
  0.0 153.9 jit_solution(5454111718752863856)
XLA Ops:
  7.3 2.9 %gather_fusion = bf16[16,256,128]{2,1,0:T(8,128)(2,1)S(1)} fusion(bf16[64,256,128]{2,1,0:T(8,128)(2,1)} %param.13, s32[1024]{0:T(1024)S(1)} %pad_clamp_fusion), kind=kCustom, calls=%fused_computation | custom fusion | bytes 2097216 | tf_op jit(solution)/shard_map/jit(_take)/gather | solution.py:58
  10.2 1.4 multiply_convert_fusion.1
  11.7 3.4 %convert_reduce_fusion = f32[64,256]{1,0:T(8,128)S(1)} fusion(bf16[64,256,128]{2,1,0:T(8,128)(2,1)} %param.13), kind=kLoop, calls=%fused_computation.3 | loop fusion | flops 4177920 | bytes 4259840 | tf_op jit(solution)/shard_map/reduce_sum | solution.py:16
  15.2 6.1 %fusion.2 = f32[64,256]{1,0:T(8,128)S(1)} fusion(bf16[64,256,128]{2,1,0:T(8,128)(2,1)} %param.13, f32[64,256]{1,0:T(8,128)S(1)} %broadcast_multiply_fusion), kind=kLoop, calls=%fused_computation.6 | loop fusion | flops 8372224 | bytes 4325376 | tf_op jit(solution)/shard_map/reduce_sum | solution.py:17
  21.4 11.2 %fusion.5 = f32[64,256,64]{1,2,0:T(8,128)S(1)} fusion(bf16[64,256,128]{2,1,0:T(8,128)(2,1)S(1)} %copy-done.1, f32[128]{0:T(128)S(1)} %copy-done.10, f32[64,256]{1,0:T(8,128)S(1)} %add_rsqrt_fusion, f32[64,256]{1,0:T(8,128)S(1)} %broadcast_multiply_fusion, bf16[128,64]{0,1:T(8,128)(2,1)S(1)} %copy-done.6), kind=kOutput, calls=%fused_computation.10 | convolution fusion | flops 278921216 | bytes 8536576 | tf_op jit(solution)/shard_map/rkd,dc->crk/dot_general | solution.py:22
  32.6 8.6 %fusion.9 = bf16[64,64,256]{2,0,1:T(8,128)(2,1)S(1)} fusion(f32[256]{0:T(256)S(1)} %dynamic_slice.10, f32[64]{0:T(128)S(1)} %dynamic_slice.11, f32[64,256,64]{1,2,0:T(8,128)S(1)} %fusion.5, bf16[64,256,128]{2,1,0:T(8,128)(2,1)S(1)} %copy-done.1, f32[128]{0:T(128)S(1)} %copy-done.10, f32[64,256]{1,0:T(8,128)S(1)} %add_rsqrt_fusion, ...), kind=kOutput, calls=%fused_computation.14 | convolution fusion | flops 286261248 | bytes 10635008 | tf_op jit(solution)/shard_map/rkd,dc->crk/dot_general | solution.py:23
  41.3 2.5 %copy.32 = bf16[64,64,256]{2,1,0:T(8,128)(2,1)} copy(bf16[64,64,256]{2,0,1:T(8,128)(2,1)S(1)} %fusion.9) | data formatting | bytes 4194304 | tf_op jit(solution)/shard_map/convert_element_type | solution.py:53
  43.8 4.2 %all-to-all-start.1 = ((bf16[64,64,256]{2,1,0:T(8,128)(2,1)}), bf16[64,64,256]{2,1,0:T(8,128)(2,1)S(1)}, u32[]{:S(2)}, u32[]{:S(2)}) async-start(bf16[64,64,256]{2,1,0:T(8,128)(2,1)} %copy.32), calls=%async_computation.2 | async-start | bytes 4194304 | tf_op jit(solution)/shard_map/all_to_all | solution.py:74
  50.3 1.3 fusion.20
  53.6 20.4 %all-to-all-done.1 = bf16[64,64,256]{2,1,0:T(8,128)(2,1)S(1)} async-done(((bf16[64,64,256]{2,1,0:T(8,128)(2,1)}), bf16[64,64,256]{2,1,0:T(8,128)(2,1)S(1)}, u32[]{:S(2)}, u32[]{:S(2)}) %all-to-all-start.1) | async-done | bytes 2097184 | tf_op jit(solution)/shard_map/all_to_all | solution.py:74
  73.9 3.3 %all-to-all-start = ((bf16[64,2,256]{2,1,0:T(2,128)(2,1)}), bf16[64,2,256]{2,1,0:T(2,128)(2,1)S(1)}, u32[]{:S(2)}, u32[]{:S(2)}) async-start(bf16[64,2,256]{2,1,0:T(2,128)(2,1)} %copy.30), calls=%async_computation.1 | async-start | bytes 131072 | tf_op jit(solution)/shard_map/all_to_all | solution.py:73
  77.2 3.5 %copy.46 = bf16[2,32,64,256]{3,0,2,1:T(2,128)(2,1)} copy(bf16[2,32,64,256]{3,2,1,0:T(8,128)(2,1)S(1)} %bitcast.68) | data formatting | bytes 4194304 | tf_op jit(solution)/shard_map/all_to_all | solution.py:74
  80.7 3.2 %all_to_all.53 = bf16[32,64,512]{2,1,0:T(8,128)(2,1)S(1)} reshape(bf16[32,64,2,256]{3,2,1,0:T(2,128)(2,1)} %bitcast.69) | data formatting | bytes 4194304 | tf_op jit(solution)/shard_map/all_to_all | solution.py:74
  84.8 43.7 %while.17 = (s32[]{:T(128)}, bf16[32,2,512]{2,1,0:T(2,128)(2,1)S(1)}, bf16[32,16,64]{2,1,0:T(8,128)(2,1)S(1)}, bf16[32,64,512]{2,1,0:T(8,128)(2,1)S(1)}, s32[]{:...) while((s32[]{:T(128)}, ...), condition=%wide.region_6.7_spmd, body=%wide.region_5.6_spmd.sunk | while | flops 4194322 | bytes 2588992 | solution.py:89
  84.8 5.5 %collective-permute-done = bf16[32,2,512]{2,1,0:T(2,128)(2,1)S(1)} collective-permute-done((bf16[32,2,512]{2,1,0:T(2,128)(2,1)S(1)}, bf16[32,2,512]{2,1,0:T(2,128)(2,1)S(1)}, u32[]{:S(2)}, u32[]{:S(2)}) %collective-permute-start) | collective-permute-done | bytes 65568 | tf_op jit(solution)/shard_map/while/body/eval_jaxpr/ppermute | solution.py:11
  91.1 5.5 %collective-permute-done = bf16[32,2,512]{2,1,0:T(2,128)(2,1)S(1)} collective-permute-done((bf16[32,2,512]{2,1,0:T(2,128)(2,1)S(1)}, bf16[32,2,512]{2,1,0:T(2,128)(2,1)S(1)}, u32[]{:S(2)}, u32[]{:S(2)}) %collective-permute-start) | collective-permute-done | bytes 65568 | tf_op jit(solution)/shard_map/while/body/eval_jaxpr/ppermute | solution.py:11
  97.3 5.5 %collective-permute-done = bf16[32,2,512]{2,1,0:T(2,128)(2,1)S(1)} collective-permute-done((bf16[32,2,512]{2,1,0:T(2,128)(2,1)S(1)}, bf16[32,2,512]{2,1,0:T(2,128)(2,1)S(1)}, u32[]{:S(2)}, u32[]{:S(2)}) %collective-permute-start) | collective-permute-done | bytes 65568 | tf_op jit(solution)/shard_map/while/body/eval_jaxpr/ppermute | solution.py:11
  103.5 5.5 %collective-permute-done = bf16[32,2,512]{2,1,0:T(2,128)(2,1)S(1)} collective-permute-done((bf16[32,2,512]{2,1,0:T(2,128)(2,1)S(1)}, bf16[32,2,512]{2,1,0:T(2,128)(2,1)S(1)}, u32[]{:S(2)}, u32[]{:S(2)}) %collective-permute-start) | collective-permute-done | bytes 65568 | tf_op jit(solution)/shard_map/while/body/eval_jaxpr/ppermute | solution.py:11
  109.8 5.5 %collective-permute-done = bf16[32,2,512]{2,1,0:T(2,128)(2,1)S(1)} collective-permute-done((bf16[32,2,512]{2,1,0:T(2,128)(2,1)S(1)}, bf16[32,2,512]{2,1,0:T(2,128)(2,1)S(1)}, u32[]{:S(2)}, u32[]{:S(2)}) %collective-permute-start) | collective-permute-done | bytes 65568 | tf_op jit(solution)/shard_map/while/body/eval_jaxpr/ppermute | solution.py:11
  116.0 5.5 %collective-permute-done = bf16[32,2,512]{2,1,0:T(2,128)(2,1)S(1)} collective-permute-done((bf16[32,2,512]{2,1,0:T(2,128)(2,1)S(1)}, bf16[32,2,512]{2,1,0:T(2,128)(2,1)S(1)}, u32[]{:S(2)}, u32[]{:S(2)}) %collective-permute-start) | collective-permute-done | bytes 65568 | tf_op jit(solution)/shard_map/while/body/eval_jaxpr/ppermute | solution.py:11
  122.2 5.5 %collective-permute-done = bf16[32,2,512]{2,1,0:T(2,128)(2,1)S(1)} collective-permute-done((bf16[32,2,512]{2,1,0:T(2,128)(2,1)S(1)}, bf16[32,2,512]{2,1,0:T(2,128)(2,1)S(1)}, u32[]{:S(2)}, u32[]{:S(2)}) %collective-permute-start) | collective-permute-done | bytes 65568 | tf_op jit(solution)/shard_map/while/body/eval_jaxpr/ppermute | solution.py:11
  128.6 8.3 %all_to_all.63 = bf16[8,2,2048]{2,1,0:T(2,128)(2,1)S(1)} all-to-all(bf16[8,2,2048]{2,1,0:T(2,128)(2,1)S(1)} %reshape.97), channel_id=1, replica_groups=mesh['group'=2,'row'=8,'chan'=2] {'row'}, dimensions={0} | all-to-all | bytes 131072 | tf_op jit(solution)/shard_map/all_to_all | solution.py:92
  138.2 3.3 %all-to-all-start.3 = ((bf16[2,2,8192]{2,1,0:T(2,128)(2,1)}), bf16[2,2,8192]{2,1,0:T(2,128)(2,1)S(1)}, u32[]{:S(2)}, u32[]{:S(2)}) async-start(bf16[2,2,8192]{2,1,0:T(2,128)(2,1)} %reshape.99), calls=%async_computation.4 | async-start | bytes 131072 | tf_op jit(solution)/shard_map/all_to_all | solution.py:91
  141.8 3.7 %all-to-all-done.3 = bf16[2,2,8192]{2,1,0:T(2,128)(2,1)S(1)} async-done(((bf16[2,2,8192]{2,1,0:T(2,128)(2,1)}), bf16[2,2,8192]{2,1,0:T(2,128)(2,1)S(1)}, u32[]{:S(2)}, u32[]{:S(2)}) %all-to-all-start.3) | async-done | bytes 65568 | tf_op jit(solution)/shard_map/all_to_all | solution.py:91
  (82 shorter events, 13.8 us)
Async XLA Ops:
  6.5 134.9 %copy-start = (bf16[128,128]{1,0:T(8,128)(2,1)S(1)}, bf16[128,128]{1,0:T(8,128)(2,1)}, u32[]{:S(2)}) copy-start(bf16[128,128]{1,0:T(8,128)(2,1)} %param.20) | copy-start | bytes 98308
  6.5 41.6 %reduce-scatter.2.cloned.1.call-start = ((), (), s32[]{:S(2)}) async-start(), calls=%async_computation.5 | async-start | bytes 1179648 | tf_op jit(solution)/shard_map/reduce_scatter | solution.py:59
  10.2 4.8 %copy-start.4 = (s32[512]{0:T(512)S(1)}, s32[512]{0:T(512)}, u32[]{:S(2)}) copy-start(s32[512]{0:T(512)} %param.14) | copy-start | bytes 6148
  11.6 9.7 %copy-start.6 = (bf16[128,64]{0,1:T(8,128)(2,1)S(1)}, bf16[128,64]{0,1:T(8,128)(2,1)}, u32[]{:S(2)}) copy-start(bf16[128,64]{0,1:T(8,128)(2,1)} %param.18) | copy-start | bytes 49156
  11.6 9.7 %copy-start.10 = (f32[128]{0:T(128)S(1)}, f32[128]{0:T(128)}, u32[]{:S(2)}) copy-start(f32[128]{0:T(128)} %param.22) | copy-start | bytes 1540
  15.1 6.3 %copy-start.1 = (bf16[64,256,128]{2,1,0:T(8,128)(2,1)S(1)}, bf16[64,256,128]{2,1,0:T(8,128)(2,1)}, u32[]{:S(2)}) copy-start(bf16[64,256,128]{2,1,0:T(8,128)(2,1)} %param.13) | copy-start | bytes 12582916
  21.4 11.2 %copy-start.7 = (bf16[128,64]{0,1:T(8,128)(2,1)S(1)}, bf16[128,64]{0,1:T(8,128)(2,1)}, u32[]{:S(2)}) copy-start(bf16[128,64]{0,1:T(8,128)(2,1)} %param.19) | copy-start | bytes 49156
  41.3 9.0 %copy-start.8 = (bf16[128,64]{0,1:T(8,128)(2,1)S(1)}, bf16[128,64]{0,1:T(8,128)(2,1)}, u32[]{:S(2)}) copy-start(bf16[128,64]{0,1:T(8,128)(2,1)} %param.17) | copy-start | bytes 49156
  41.3 10.3 %copy-start.9 = (bf16[128,64]{0,1:T(8,128)(2,1)S(1)}, bf16[128,64]{0,1:T(8,128)(2,1)}, u32[]{:S(2)}) copy-start(bf16[128,64]{0,1:T(8,128)(2,1)} %param.16) | copy-start | bytes 49156
  43.8 30.1 %all-to-all-start.1 = ((bf16[64,64,256]{2,1,0:T(8,128)(2,1)}), bf16[64,64,256]{2,1,0:T(8,128)(2,1)S(1)}, u32[]{:S(2)}, u32[]{:S(2)}) async-start(bf16[64,64,256]{2,1,0:T(8,128)(2,1)} %copy.32), calls=%async_computation.2 | async-start | bytes 4194304 | tf_op jit(solution)/shard_map/all_to_all | solution.py:74
  73.9 10.0 %all-to-all-start = ((bf16[64,2,256]{2,1,0:T(2,128)(2,1)}), bf16[64,2,256]{2,1,0:T(2,128)(2,1)S(1)}, u32[]{:S(2)}, u32[]{:S(2)}) async-start(bf16[64,2,256]{2,1,0:T(2,128)(2,1)} %copy.30), calls=%async_computation.1 | async-start | bytes 131072 | tf_op jit(solution)/shard_map/all_to_all | solution.py:73
  84.7 56.7 %copy-start.2 = (bf16[2,256,128]{2,1,0:T(8,128)(2,1)S(1)}, bf16[2,256,128]{2,1,0:T(8,128)(2,1)}, u32[]{:S(2)}) copy-start(bf16[2,256,128]{2,1,0:T(8,128)(2,1)} %reduce-scatter.2.cloned.1.call-done) | copy-start | bytes 393220
  84.8 5.5 %collective-permute-start = (bf16[32,2,512]{2,1,0:T(2,128)(2,1)S(1)}, bf16[32,2,512]{2,1,0:T(2,128)(2,1)S(1)}, u32[]{:S(2)}, u32[]{:S(2)}) collective-permute-start(bf16[32,2,512]{2,1,0:T(2,128)(2,1)S(1)} %get-tuple-element.194), channel_id=1, source_target_pairs={{0,2},{2,4},{4,6},{6,8},{8,10},{10,12},{12,14},{14,0},{1,3},{3,5},... | collective-permute-start | bytes 196616 | tf_op jit(solution)/shard_map/while/body/eval_jaxpr/ppermute | solution.py:11
  91.0 5.5 %collective-permute-start = (bf16[32,2,512]{2,1,0:T(2,128)(2,1)S(1)}, bf16[32,2,512]{2,1,0:T(2,128)(2,1)S(1)}, u32[]{:S(2)}, u32[]{:S(2)}) collective-permute-start(bf16[32,2,512]{2,1,0:T(2,128)(2,1)S(1)} %get-tuple-element.194), channel_id=1, source_target_pairs={{0,2},{2,4},{4,6},{6,8},{8,10},{10,12},{12,14},{14,0},{1,3},{3,5},... | collective-permute-start | bytes 196616 | tf_op jit(solution)/shard_map/while/body/eval_jaxpr/ppermute | solution.py:11
  97.2 5.5 %collective-permute-start = (bf16[32,2,512]{2,1,0:T(2,128)(2,1)S(1)}, bf16[32,2,512]{2,1,0:T(2,128)(2,1)S(1)}, u32[]{:S(2)}, u32[]{:S(2)}) collective-permute-start(bf16[32,2,512]{2,1,0:T(2,128)(2,1)S(1)} %get-tuple-element.194), channel_id=1, source_target_pairs={{0,2},{2,4},{4,6},{6,8},{8,10},{10,12},{12,14},{14,0},{1,3},{3,5},... | collective-permute-start | bytes 196616 | tf_op jit(solution)/shard_map/while/body/eval_jaxpr/ppermute | solution.py:11
  103.5 5.5 %collective-permute-start = (bf16[32,2,512]{2,1,0:T(2,128)(2,1)S(1)}, bf16[32,2,512]{2,1,0:T(2,128)(2,1)S(1)}, u32[]{:S(2)}, u32[]{:S(2)}) collective-permute-start(bf16[32,2,512]{2,1,0:T(2,128)(2,1)S(1)} %get-tuple-element.194), channel_id=1, source_target_pairs={{0,2},{2,4},{4,6},{6,8},{8,10},{10,12},{12,14},{14,0},{1,3},{3,5},... | collective-permute-start | bytes 196616 | tf_op jit(solution)/shard_map/while/body/eval_jaxpr/ppermute | solution.py:11
  109.7 5.5 %collective-permute-start = (bf16[32,2,512]{2,1,0:T(2,128)(2,1)S(1)}, bf16[32,2,512]{2,1,0:T(2,128)(2,1)S(1)}, u32[]{:S(2)}, u32[]{:S(2)}) collective-permute-start(bf16[32,2,512]{2,1,0:T(2,128)(2,1)S(1)} %get-tuple-element.194), channel_id=1, source_target_pairs={{0,2},{2,4},{4,6},{6,8},{8,10},{10,12},{12,14},{14,0},{1,3},{3,5},... | collective-permute-start | bytes 196616 | tf_op jit(solution)/shard_map/while/body/eval_jaxpr/ppermute | solution.py:11
  115.9 5.5 %collective-permute-start = (bf16[32,2,512]{2,1,0:T(2,128)(2,1)S(1)}, bf16[32,2,512]{2,1,0:T(2,128)(2,1)S(1)}, u32[]{:S(2)}, u32[]{:S(2)}) collective-permute-start(bf16[32,2,512]{2,1,0:T(2,128)(2,1)S(1)} %get-tuple-element.194), channel_id=1, source_target_pairs={{0,2},{2,4},{4,6},{6,8},{8,10},{10,12},{12,14},{14,0},{1,3},{3,5},... | collective-permute-start | bytes 196616 | tf_op jit(solution)/shard_map/while/body/eval_jaxpr/ppermute | solution.py:11
  122.2 5.5 %collective-permute-start = (bf16[32,2,512]{2,1,0:T(2,128)(2,1)S(1)}, bf16[32,2,512]{2,1,0:T(2,128)(2,1)S(1)}, u32[]{:S(2)}, u32[]{:S(2)}) collective-permute-start(bf16[32,2,512]{2,1,0:T(2,128)(2,1)S(1)} %get-tuple-element.194), channel_id=1, source_target_pairs={{0,2},{2,4},{4,6},{6,8},{8,10},{10,12},{12,14},{14,0},{1,3},{3,5},... | collective-permute-start | bytes 196616 | tf_op jit(solution)/shard_map/while/body/eval_jaxpr/ppermute | solution.py:11
  128.4 17.7 %copy-start.5 = (f32[64]{0:T(128)S(1)}, f32[64]{0:T(128)}, u32[]{:S(2)}) copy-start(f32[64]{0:T(128)} %param.23) | copy-start | bytes 772
  128.4 17.8 %copy-start.3 = (bf16[64,128]{1,0:T(8,128)(2,1)S(1)}, bf16[64,128]{1,0:T(8,128)(2,1)}, u32[]{:S(2)}) copy-start(bf16[64,128]{1,0:T(8,128)(2,1)} %param.21) | copy-start | bytes 49156
  138.2 7.4 %all-to-all-start.3 = ((bf16[2,2,8192]{2,1,0:T(2,128)(2,1)}), bf16[2,2,8192]{2,1,0:T(2,128)(2,1)S(1)}, u32[]{:S(2)}, u32[]{:S(2)}) async-start(bf16[2,2,8192]{2,1,0:T(2,128)(2,1)} %reshape.99), calls=%async_computation.4 | async-start | bytes 131072 | tf_op jit(solution)/shard_map/all_to_all | solution.py:91
Sparse Core Ops, SparseCore 0:
  11.7 34.9 reduce-scatter.1
where the time goes:
time: 155 us; the launch traced here: 154 us
  waiting for transfers between devices  62.3 us (40%)
  matrix products  28.9 us (19%)
  local copies, waits for them, and re-layouts  15.5 us (10%)
  between operations  14.4 us (9%)
  other arithmetic  13.3 us (9%)
  starting transfers between devices  11 us (7%)
  blocking collectives  8.3 us (5%)
    ppermute x7, waiting for transfers between devices, from_behind(): lax.ppermute(shard, axis, [(i, (i + by) % size) for i in range(size)])  38.2 us
    all_to_all x1, waiting for transfers between devices, body(): lax.all_to_all(right, 'chan', split_axis=0, concat_axis=2, tiled=True)  20.4 us
    dot_general x2, matrix products, channel_gated(): jnp.einsum('rkd,dc->crk', normed, w_value, preferred_element_type=jnp.flo...  12.4 us
    dot_general x2, matrix products, channel_gated(): jnp.einsum('rkd,dc->crk', normed, w_gate, preferred_element_type=jnp.floa...  9.92 us
    all_to_all x1, blocking collectives, body(): lax.all_to_all(product, 'row', split_axis=1, concat_axis=2, tiled=True)  8.3 us
    reduce_sum x3, other arithmetic, layer_norm(): spread = jnp.mean(jnp.square(values - middle), -1, keepdims=True)  7.32 us
    all_to_all x2, local copies, waits for them, and re-layouts, body(): lax.all_to_all(right, 'chan', split_axis=0, concat_axis=2, tiled=True)  6.68 us
    dot_general x8, matrix products, block_product(): jnp.einsum('cik,cjk->cij', block, right_cols, preferred_element_type=jnp....  5.37 us
  transfers between devices with their start and end apart: 11, of which 9 were waited for; matrix products, arithmetic and copies ran while one was open for 27% of the time, Pallas kernels for 0%

commit v1 on v0

v1 whole, which is shorter than its diff:
```python
import functools

import jax
import jax.numpy as jnp
from jax import lax
from jax.experimental import pallas as pl
from jax.experimental.pallas import tpu as pltpu
from jax.sharding import PartitionSpec as P

BAND_DEV = 2
MESH = pl.DeviceIdType.MESH
F32 = jnp.float32
BF16 = jnp.bfloat16


def dot(a, b):
    return jnp.dot(a, b, preferred_element_type=F32)


def sigmoid(x):
    return 0.5 + 0.5 * jnp.tanh(0.5 * x)


def normalise(x, mean_w, gain):
    xc = x.astype(F32) - dot(x, mean_w)
    var = dot((xc * xc).astype(BF16), mean_w)
    return (xc * lax.rsqrt(var + 1e-05) * gain).astype(BF16)


def kernel(
    R,
    LN,
    start_ref,
    pair,
    col_valid,
    row_valid,
    left_valid,
    mean_in,
    gain_in,
    w_right2,
    w_left2,
    w_gate,
    mean_out,
    gain_out,
    w_out2,
    out,
    right,
    send_a,
    recv_a,
    send_b,
    recv_b,
    left_all,
    left_dup,
    gate,
    partial,
    p_send,
    p_recv,
    a_sem,
    b_send_sem,
    b_recv_sem,
    l_send_sem,
    f_send_sem,
    l_recv_sem,
    p_send_sem,
    p_recv_sem,
):
    rows_dev, cols, width = pair.shape
    half = rows_dev // 2
    CH = width // 2
    Z = R // 2
    me = lax.axis_index("row")
    lane = lax.axis_index("chan")
    z, core = me // 2, me % 2
    sib = me + 1 - 2 * core
    start = start_ref[0]

    def at(row, chan=None):
        if chan is None:
            return {"row": row}
        return {"row": row, "chan": chan}

    barrier = pltpu.get_barrier_semaphore()
    flat = me * LN + lane

    def greet(i, _):
        other = (flat + i) % (R * LN)
        pl.semaphore_signal(barrier, inc=1, device_id=at(other // LN, other % LN), device_id_type=MESH)
        return 0

    lax.fori_loop(1, R * LN, greet, 0)

    def candidate(t):
        return pair[jnp.clip(start + t - me * rows_dev, 0, rows_dev - 1)]

    def fill_a(i, _):
        t = (i // 2) * 4 + (1 - core) * 2 + i % 2
        send_a[i] = candidate(t)
        return 0

    lax.fori_loop(0, R, fill_a, 0)

    pl.semaphore_wait(barrier, R * LN - 1)
    copy_a = pltpu.make_async_remote_copy(
        src_ref=send_a, dst_ref=recv_a, send_sem=a_sem.at[0], recv_sem=a_sem.at[1],
        device_id=at(sib), device_id_type=MESH,
    )
    copy_a.start()

    g_in = gain_in[...]

    def right_rows(jp):
        x = jnp.concatenate([pair[jp], pair[jp + half]], axis=1)
        both = dot(normalise(x, mean_in[...], g_in), w_right2[...])
        right[jp] = sigmoid(both[:, width:]) * both[:, :width]

    def right_loop(lo, hi):
        def step(i, _):
            right_rows(lo + 2 * i)
            right_rows(lo + 2 * i + 1)
            return 0

        lax.fori_loop(0, (hi - lo) // 2, step, 0)

    right_loop(0, half // 8)
    copy_a.wait_recv()

    def fill_b(i, _):
        t = (i // 2) * 4 + core * 2 + i % 2
        theirs = ((start + t) // rows_dev == sib).astype(F32)
        mix = recv_a[i].astype(F32) * theirs + candidate(t).astype(F32) * (1.0 - theirs)
        send_b[i // 2, i % 2] = mix.astype(BF16)
        return 0

    lax.fori_loop(0, R, fill_b, 0)

    def copy_b(i):
        peer = (z + i) % Z
        return pltpu.make_async_remote_copy(
            src_ref=send_b.at[peer], dst_ref=recv_b.at[z],
            send_sem=b_send_sem.at[i], recv_sem=b_recv_sem.at[i],
            device_id=at(peer * 2 + core), device_id_type=MESH,
        )

    for i in range(1, Z):
        copy_b(i).start()
    recv_b[z] = send_b[z]
    right_loop(half // 8, half)
    for i in range(1, Z):
        copy_b(i).wait_recv()

    t = me * BAND_DEV
    rows = [recv_b[(start + t + i) // (2 * rows_dev), i] for i in range(2)]
    normed = normalise(jnp.concatenate(rows, axis=1), mean_in[...], g_in)
    both = dot(normed, w_left2[...])
    factor = sigmoid(both[:, width:]) * both[:, :width] * left_valid[...] * col_valid[...]
    left_all[me] = factor.astype(BF16)

    def copy_l(i):
        peer = ((z + i) % Z) * 2 + core
        return pltpu.make_async_remote_copy(
            src_ref=left_all.at[me], dst_ref=left_all.at[me],
            send_sem=l_send_sem.at[i], recv_sem=l_recv_sem.at[i, 0],
            device_id=at(sib if i == 0 else peer), device_id_type=MESH,
        )

    def forward(i):
        slot = ((z + Z - i) % Z) * 2 + core
        return pltpu.make_async_remote_copy(
            src_ref=left_all.at[slot], dst_ref=left_all.at[slot],
            send_sem=f_send_sem.at[i], recv_sem=l_recv_sem.at[i, 1],
            device_id=at(sib), device_id_type=MESH,
        )

    for i in range(1, Z):
        copy_l(i).start()
    copy_l(0).start()
    for i in range(2):
        gate[i] = sigmoid(dot(normed[:, i * width:(i + 1) * width], w_gate[...])).astype(BF16)

    low = lax.broadcasted_iota(jnp.int32, (cols, width), 1) < CH
    home = me // (R // LN)
    slot_out = (me % (R // LN)) * LN + lane

    def p_copy(s, send_slot):
        return pltpu.make_async_remote_copy(
            src_ref=p_send.at[s], dst_ref=p_recv.at[slot_out],
            send_sem=p_send_sem.at[s], recv_sem=p_recv_sem.at[slot_out],
            device_id=at(s, home), device_id_type=MESH,
        )

    def is_self(s):
        return jnp.logical_and(s == me, home == lane)

    def group_product(zz):
        for b in range(2):
            x = left_all[zz * 2 + b].astype(F32)
            turned = pltpu.roll(x, CH, 1)
            left_dup[2 * b] = jnp.where(low, x, turned)
            left_dup[2 * b + 1] = jnp.where(low, turned, x)

        def step(jg, _):
            def part(kc, acc):
                acc = list(acc)
                for k8 in range(8):
                    here = pl.ds(pl.multiple_of(kc * 64 + k8 * 8, 8), 8)
                    ls = [left_dup[a, here] for a in range(4)]
                    rs = [right[jg * 4 + b, here] for b in range(4)]
                    for a in range(4):
                        for b in range(4):
                            acc[4 * a + b] = acc[4 * a + b] + ls[a] * rs[b]
                return tuple(acc)

            acc = lax.fori_loop(0, cols // 64, part, (jnp.zeros((8, width), F32),) * 16)
            for a in range(4):
                for b in range(4):
                    partial[a, jg * 4 + b] = acc[4 * a + b]
            return 0

        lax.fori_loop(0, half // 4, step, 0)
        for b in range(2):
            s = zz * 2 + b
            for i in range(2):
                total = jnp.sum(partial[2 * b + i], axis=1) * row_valid[...]
                p_send[s, i] = total.astype(BF16)

            @pl.when(is_self(s))
            def _():
                p_recv[slot_out] = p_send[s]

            @pl.when(jnp.logical_not(is_self(s)))
            def _():
                p_copy(s, b).start()

    copy_l(0).wait_recv()
    group_product(z)
    for i in range(1, Z):
        copy_l(i).wait_recv()
        forward(i).start()

    def rest(i, _):
        forward(i).wait_recv()
        group_product((z + Z - i) % Z)
        return 0

    lax.fori_loop(1, Z, rest, 0)

    own_slot = jnp.where(home == lane, slot_out, R)
    for src in range(R // LN):
        total = None
        for other in range(LN):
            q = src * LN + other

            @pl.when(q != own_slot)
            def _():
                pltpu.make_async_remote_copy(
                    src_ref=p_send.at[0], dst_ref=p_recv.at[q],
                    send_sem=p_send_sem.at[0], recv_sem=p_recv_sem.at[q],
                    device_id=at(sib), device_id_type=MESH,
                ).wait_recv()

            piece = p_recv[q].astype(F32)
            total = piece if total is None else total + piece
        product = total.astype(BF16).reshape(2 * half, width)
        normed_p = normalise(product, mean_out[...], gain_out[...])
        projected = dot(normed_p, w_out2[...])
        for i in range(2):
            for h in range(2):
                here = slice(src * rows_dev + h * half, src * rows_dev + (h + 1) * half)
                opener = gate[i, here].astype(F32)
                mine = projected[i * half:(i + 1) * half, h * width:(h + 1) * width]
                out[i, here] = (mine * opener).astype(BF16)

    copy_a.wait_send()
    for i in range(1, Z):
        copy_b(i).wait_send()
        copy_l(i).wait_send()
        forward(i).wait_send()
    copy_l(0).wait_send()

    def drain(s, _):
        @pl.when(jnp.logical_not(is_self(s)))
        def _():
            p_copy(s, 0).wait_send()

        return 0

    lax.fori_loop(0, R, drain, 0)


def twice(a):
    zero = jnp.zeros_like(a)
    return jnp.concatenate([jnp.concatenate([a, zero], 1), jnp.concatenate([zero, a], 1)], 0)


def body(
    R,
    LN,
    pair,
    token_mask,
    band_start,
    w_left,
    w_left_gate,
    w_right,
    w_right_gate,
    w_gate_out,
    w_out,
    norm_in_gain,
    norm_out_gain,
):
    rows_dev, cols, width = pair.shape
    half = rows_dev // 2
    CH = width // 2
    place = lax.axis_index("row")
    lane = lax.axis_index("chan")
    valid = token_mask.astype(F32)
    row_valid = lax.dynamic_slice_in_dim(valid, place * rows_dev, rows_dev)
    col_valid = lax.dynamic_slice_in_dim(valid, lane * cols, cols)
    left_valid = lax.dynamic_slice_in_dim(valid, band_start[0] + place * BAND_DEV, BAND_DEV)
    col_valid = jnp.broadcast_to(col_valid[:, None], (cols, width))
    row_valid = jnp.repeat(row_valid.reshape(2, half).T, CH, axis=1)
    left_valid = jnp.repeat(left_valid, CH)[None, :]
    mean_in = twice(jnp.full((width, width), 1 / width, BF16))
    mean_out = twice(jnp.full((CH, CH), 1 / CH, BF16))
    gain_in = jnp.tile(norm_in_gain, 2)[None, :]
    gain_out = jnp.tile(norm_out_gain, 2)[None, :]
    w_right2 = jnp.concatenate([twice(w_right), twice(w_right_gate)], 1)
    w_left2 = jnp.concatenate([twice(w_left), twice(w_left_gate)], 1)
    Z = R // 2
    dma = pltpu.SemaphoreType.DMA
    vmem = pl.BlockSpec(memory_space=pltpu.VMEM)
    return pl.pallas_call(
        functools.partial(kernel, R, LN),
        out_shape=jax.ShapeDtypeStruct((BAND_DEV, cols, width), BF16),
        in_specs=[pl.BlockSpec(memory_space=pltpu.SMEM)] + [vmem] * 12,
        out_specs=vmem,
        scratch_shapes=[
            pltpu.VMEM((half, cols, width), F32),
            pltpu.VMEM((R, cols, width), BF16),
            pltpu.VMEM((R, cols, width), BF16),
            pltpu.VMEM((Z, 2, cols, width), BF16),
            pltpu.VMEM((Z, 2, cols, width), BF16),
            pltpu.VMEM((R, cols, width), BF16),
            pltpu.VMEM((4, cols, width), F32),
            pltpu.VMEM((2, cols, width), BF16),
            pltpu.VMEM((4, half, 8, width), F32),
            pltpu.VMEM((R, 2, half, width), BF16),
            pltpu.VMEM((R, 2, half, width), BF16),
            dma((2,)),
            dma((Z,)),
            dma((Z,)),
            dma((Z,)),
            dma((Z,)),
            dma((Z, 2)),
            dma((R,)),
            dma((R,)),
        ],
        compiler_params=pltpu.CompilerParams(
            collective_id=0, has_side_effects=True, vmem_limit_bytes=56 * 2**20
        ),
    )(
        band_start, pair, col_valid, row_valid, left_valid, mean_in, gain_in,
        w_right2, w_left2, w_gate_out, mean_out, gain_out, twice(w_out),
    )


def solution(mesh):
    R, LN = mesh.shape["row"], mesh.shape["chan"]
    return jax.shard_map(
        functools.partial(body, R, LN),
        mesh=mesh,
        in_specs=(
            P(("group", "row"), "chan", None),
            P("group"),
            P("group"),
            P(),
            P(),
            P(),
            P(),
            P(),
            P(),
            P(),
            P(),
        ),
        out_specs=P(("group", "row"), "chan", None),
        check_vma=False,
    )
```

time: 155 us -> 53.8 us (0.35)
  the two profiles are of different devices: /device:TPU:0 before, /device:TPU:3 now
where the time goes in v1:
time: 53.8 us; the launch traced here: 53.1 us
  Pallas kernels  39.5 us (73%)
  local copies, waits for them, and re-layouts  10 us (19%)
  other arithmetic  2.92 us (5%)
  between operations  0.69 us (1%)
    pallas_call x1, Pallas kernels, body(): pl.pallas_call(functools.partial(kernel, R, LN), out_shape=jax.ShapeDtype...  39.5 us
    unnamed x5, local copies, waits for them, and re-layouts  4.89 us
    concatenate x1, other arithmetic, twice(): jnp.concatenate([jnp.concatenate([a, zero], 1), jnp.concatenate([zero, a]...  1.42 us
    another operation x2, local copies, waits for them, and re-layouts, body(): gain_out = jnp.tile(norm_out_gain, 2)[None, :]  1.24 us
    another operation x1, local copies, waits for them, and re-layouts, body(): gain_in = jnp.tile(norm_in_gain, 2)[None, :]  1.22 us

profile of v1, /device:TPU:3, one launch (start us, length us, event | category | flops | bytes accessed | tf_op | source)
XLA Modules:
  0.0 53.1 jit_solution(289807137803018170)
XLA Ops:
  0.7 0.7 %convert_element_type.3 = f32[512]{0:T(512)S(1)} convert(s32[512]{0:T(512)} %param.12) | non-fusion elementwise | flops 512 | bytes 4096 | tf_op jit(solution)/shard_map/convert_element_type | solution.py:315
  1.3 0.1 dynamic_slice.11
  1.4 0.1 broadcast_in_dim.15
  1.5 0.7 %broadcast_in_dim_reshape.3.left_valid = f32[1,128]{1,0:T(1,128)} reshape(f32[2,64]{1,0:T(2,128)S(1)} %broadcast_in_dim.15) | data formatting | bytes 1024 | tf_op jit(solution)/shard_map/broadcast_in_dim;reshape | solution.py:321
  2.2 0.1 dynamic_slice.10
  2.2 0.1 reshape.9
  2.3 0.1 copy.12
  2.4 0.1 broadcast_in_dim.14
  2.5 0.7 %reshape.10.row_valid = f32[32,128]{1,0:T(8,128)} reshape(f32[32,2,64]{2,1,0:T(2,128)S(1)} %broadcast_in_dim.14) | data formatting | bytes 32768 | tf_op jit(solution)/shard_map/reshape | solution.py:320
  3.2 0.1 dynamic_slice.9
  3.3 0.8 %broadcast_in_dim.6.col_valid = f32[256,128]{1,0:T(8,128)} broadcast(f32[256]{0:T(256)S(1)} %dynamic_slice.9), dimensions={0} | broadcast | bytes 132096 | tf_op jit(solution)/shard_map/broadcast_in_dim | solution.py:319
  4.0 0.8 %copy.13 = bf16[128,64]{1,0:T(8,128)(2,1)S(1)} copy(bf16[128,64]{0,1:T(8,128)(2,1)} %param.16) | data formatting | bytes 32768 | tf_op args[5]
  4.9 0.8 %copy.15 = bf16[128,64]{1,0:T(8,128)(2,1)S(1)} copy(bf16[128,64]{0,1:T(8,128)(2,1)} %param.17) | data formatting | bytes 32768 | tf_op args[6]
  5.7 0.8 %copy.17 = bf16[128,64]{1,0:T(8,128)(2,1)S(1)} copy(bf16[128,64]{0,1:T(8,128)(2,1)} %param.14) | data formatting | bytes 32768 | tf_op args[3]
  6.5 0.8 %copy.19 = bf16[128,64]{1,0:T(8,128)(2,1)S(1)} copy(bf16[128,64]{0,1:T(8,128)(2,1)} %param.15) | data formatting | bytes 32768 | tf_op args[4]
  7.4 0.8 %fusion.21 = (bf16[256,256]{1,0:T(8,128)(2,1)}, bf16[256,256]{1,0:T(8,128)(2,1)}) fusion(bf16[128,64]{1,0:T(8,128)(2,1)S(1)} %copy.15, bf16[128,64]{1,0:T(8,128)(2,1)S(1)} %copy.13, bf16[128,64]{1,0:T(8,128)(2,1)S(1)} %copy.19, bf16[128,64]{1,0:T(8,128)(2,1)S(1)} %copy.17), kind=kLoop, calls=%fused_computation.25 | loop fusion | flops 2621440 | bytes 327680 | tf_op jit(solution)/shard_map/concatenate | solution.py:326
  8.2 1.4 %fusion.28.w_out2 = bf16[128,256]{1,0:T(8,128)(2,1)} fusion(bf16[64,128]{1,0:T(8,128)(2,1)} %param.19), kind=kLoop, calls=%fused_computation.34 | loop fusion | flops 262144 | bytes 81920 | tf_op jit(solution)/shard_map/concatenate | solution.py:292
  9.6 0.7 %tile.5 = f32[2,64]{1,0:T(2,128)S(1)} broadcast(f32[64]{0:T(128)} %param.21), dimensions={1} | broadcast | bytes 768 | tf_op jit(solution)/shard_map/tile | solution.py:325
  10.3 0.6 %broadcast_in_dim_tile.7.gain_out = f32[1,128]{1,0:T(1,128)} reshape(f32[2,64]{1,0:T(2,128)S(1)} %tile.5) | data formatting | bytes 1024 | tf_op jit(solution)/shard_map/broadcast_in_dim;tile | solution.py:325
  10.8 1.2 %tile.4 = f32[2,128]{1,0:T(2,128)} broadcast(f32[128]{0:T(128)} %param.20), dimensions={1} | broadcast | bytes 1536 | tf_op jit(solution)/shard_map/tile | solution.py:324
  12.1 39.5 %shard_map.109 = bf16[2,256,128]{2,1,0:T(8,128)(2,1)} custom-call(s32[1]{0:T(128)} %copy.22.start_ref, bf16[64,256,128]{2,1,0:T(8,128)(2,1)} %pair.1, f32[256,128]{1,0:T(8,128)} %broadcast_in_dim.6.col_valid, f32[32,128]{1,0:T(8,128)} %reshape.10.row_valid, f32[1,128]{1,0:T(1,128)} %broadcast_in_dim_reshape.3.left_valid, ...), custom_call_target="tpu_custom_call" | custom-call | tf_op jit(solution)/shard_map/pallas_call | solution.py:331
  51.5 1.6 %copy.23 = bf16[2,256,128]{2,1,0:T(8,128)(2,1)} copy(bf16[2,256,128]{2,1,0:T(8,128)(2,1)} %shard_map.109) | data formatting | bytes 262144

commit v2 on v1

--- a/solution.py
+++ b/solution.py
@@ -31,18 +31,16 @@
     R,
     LN,
     start_ref,
-    pair,
-    col_valid,
-    row_valid,
-    left_valid,
-    mean_in,
-    gain_in,
-    w_right2,
-    w_left2,
+    mask_ref,
+    pair_hbm,
+    w_left_t,
+    w_left_gate_t,
+    w_right_t,
+    w_right_gate_t,
     w_gate,
-    mean_out,
-    gain_out,
-    w_out2,
+    w_out,
+    gain_in_ref,
+    gain_out_ref,
     out,
     right,
     send_a,
@@ -55,6 +53,14 @@
     partial,
     p_send,
     p_recv,
+    pair,
+    col_valid,
+    row_valid,
+    mean_in,
+    mean_out,
+    w_right2,
+    w_left2,
+    pair_sem,
     a_sem,
     b_send_sem,
     b_recv_sem,
@@ -79,6 +85,9 @@
             return {"row": row}
         return {"row": row, "chan": chan}
 
+    load = pltpu.make_async_copy(pair_hbm, pair, pair_sem)
+    load.start()
+
     barrier = pltpu.get_barrier_semaphore()
     flat = me * LN + lane
 
@@ -89,6 +98,49 @@
 
     lax.fori_loop(1, R * LN, greet, 0)
 
+    def same_block(size, block):
+        i = lax.broadcasted_iota(jnp.int32, (size, size), 0) // block
+        j = lax.broadcasted_iota(jnp.int32, (size, size), 1) // block
+        return jnp.where(i == j, 1.0 / block, 0.0).astype(BF16)
+
+    def pair_weights(value_t, gate_t):
+        zero = jnp.zeros((CH, width), BF16)
+        parts = [(value_t, zero), (zero, value_t), (gate_t, zero), (zero, gate_t)]
+        return jnp.concatenate([jnp.concatenate(p, 1) for p in parts], 0).T
+
+    mean_in[...] = same_block(2 * width, width)
+    mean_out[...] = same_block(width, CH)
+    w_right2[...] = pair_weights(w_right_t[...], w_right_gate_t[...])
+    w_left2[...] = pair_weights(w_left_t[...], w_left_gate_t[...])
+    tokens = mask_ref.shape[1]
+    valid = mask_ref[...].astype(F32)
+    ones = jnp.ones((tokens, width), BF16)
+
+    def picked(count, first):
+        token = lax.broadcasted_iota(jnp.int32, (count, tokens), 1)
+        wanted = lax.broadcasted_iota(jnp.int32, (count, tokens), 0) + first
+        return dot(jnp.where(token == wanted, valid, 0.0).astype(BF16), ones)
+
+    col_valid[...] = picked(cols, lane * cols)
+    left_half = lax.broadcasted_iota(jnp.int32, (half, width), 1) < CH
+    row_valid[...] = jnp.where(
+        left_half, picked(half, me * rows_dev), picked(half, me * rows_dev + half)
+    )
+    band_token = lax.broadcasted_iota(jnp.int32, (1, tokens), 1) - start - me * BAND_DEV
+    band_valid = [
+        jnp.sum(jnp.where(band_token == i, valid, 0.0), axis=1, keepdims=True) for i in range(2)
+    ]
+    left_valid = jnp.where(
+        lax.broadcasted_iota(jnp.int32, (1, width), 1) < CH, band_valid[0], band_valid[1]
+    )
+    g_in = jnp.concatenate([gain_in_ref[...]] * 2, axis=1)
+    g_out = jnp.concatenate([gain_out_ref[...]] * 2, axis=1)
+    zero_out = jnp.zeros((CH, width), BF16)
+    w_out2 = jnp.concatenate(
+        [jnp.concatenate([w_out[...], zero_out], 1), jnp.concatenate([zero_out, w_out[...]], 1)], 0
+    )
+    load.wait()
+
     def candidate(t):
         return pair[jnp.clip(start + t - me * rows_dev, 0, rows_dev - 1)]
 
@@ -105,8 +157,6 @@
         device_id=at(sib), device_id_type=MESH,
     )
     copy_a.start()
-
-    g_in = gain_in[...]
 
     def right_rows(jp):
         x = jnp.concatenate([pair[jp], pair[jp + half]], axis=1)
@@ -152,7 +202,7 @@
     rows = [recv_b[(start + t + i) // (2 * rows_dev), i] for i in range(2)]
     normed = normalise(jnp.concatenate(rows, axis=1), mean_in[...], g_in)
     both = dot(normed, w_left2[...])
-    factor = sigmoid(both[:, width:]) * both[:, :width] * left_valid[...] * col_valid[...]
+    factor = sigmoid(both[:, width:]) * both[:, :width] * left_valid * col_valid[...]
     left_all[me] = factor.astype(BF16)
 
     def copy_l(i):
@@ -261,8 +311,8 @@
             piece = p_recv[q].astype(F32)
             total = piece if total is None else total + piece
         product = total.astype(BF16).reshape(2 * half, width)
-        normed_p = normalise(product, mean_out[...], gain_out[...])
-        projected = dot(normed_p, w_out2[...])
+        normed_p = normalise(product, mean_out[...], g_out)
+        projected = dot(normed_p, w_out2)
         for i in range(2):
             for h in range(2):
                 here = slice(src * rows_dev + h * half, src * rows_dev + (h + 1) * half)
@@ -285,11 +335,6 @@
         return 0
 
     lax.fori_loop(0, R, drain, 0)
-
-
-def twice(a):
-    zero = jnp.zeros_like(a)
-    return jnp.concatenate([jnp.concatenate([a, zero], 1), jnp.concatenate([zero, a], 1)], 0)
 
 
 def body(
@@ -310,28 +355,13 @@
     rows_dev, cols, width = pair.shape
     half = rows_dev // 2
     CH = width // 2
-    place = lax.axis_index("row")
-    lane = lax.axis_index("chan")
-    valid = token_mask.astype(F32)
-    row_valid = lax.dynamic_slice_in_dim(valid, place * rows_dev, rows_dev)
-    col_valid = lax.dynamic_slice_in_dim(valid, lane * cols, cols)
-    left_valid = lax.dynamic_slice_in_dim(valid, band_start[0] + place * BAND_DEV, BAND_DEV)
-    col_valid = jnp.broadcast_to(col_valid[:, None], (cols, width))
-    row_valid = jnp.repeat(row_valid.reshape(2, half).T, CH, axis=1)
-    left_valid = jnp.repeat(left_valid, CH)[None, :]
-    mean_in = twice(jnp.full((width, width), 1 / width, BF16))
-    mean_out = twice(jnp.full((CH, CH), 1 / CH, BF16))
-    gain_in = jnp.tile(norm_in_gain, 2)[None, :]
-    gain_out = jnp.tile(norm_out_gain, 2)[None, :]
-    w_right2 = jnp.concatenate([twice(w_right), twice(w_right_gate)], 1)
-    w_left2 = jnp.concatenate([twice(w_left), twice(w_left_gate)], 1)
     Z = R // 2
     dma = pltpu.SemaphoreType.DMA
     vmem = pl.BlockSpec(memory_space=pltpu.VMEM)
     return pl.pallas_call(
         functools.partial(kernel, R, LN),
         out_shape=jax.ShapeDtypeStruct((BAND_DEV, cols, width), BF16),
-        in_specs=[pl.BlockSpec(memory_space=pltpu.SMEM)] + [vmem] * 12,
+        in_specs=[pl.BlockSpec(memory_space=pltpu.SMEM), vmem, pl.BlockSpec(memory_space=pl.ANY)] + [vmem] * 8,
         out_specs=vmem,
         scratch_shapes=[
             pltpu.VMEM((half, cols, width), F32),
@@ -345,6 +375,14 @@
             pltpu.VMEM((4, half, 8, width), F32),
             pltpu.VMEM((R, 2, half, width), BF16),
             pltpu.VMEM((R, 2, half, width), BF16),
+            pltpu.VMEM((rows_dev, cols, width), BF16),
+            pltpu.VMEM((cols, width), F32),
+            pltpu.VMEM((half, width), F32),
+            pltpu.VMEM((2 * width, 2 * width), BF16),
+            pltpu.VMEM((width, width), BF16),
+            pltpu.VMEM((2 * width, 2 * width), BF16),
+            pltpu.VMEM((2 * width, 2 * width), BF16),
+            dma,
             dma((2,)),
             dma((Z,)),
             dma((Z,)),
@@ -358,8 +396,8 @@
             collective_id=0, has_side_effects=True, vmem_limit_bytes=56 * 2**20
         ),
     )(
-        band_start, pair, col_valid, row_valid, left_valid, mean_in, gain_in,
-        w_right2, w_left2, w_gate_out, mean_out, gain_out, twice(w_out),
+        band_start, token_mask[None], pair, w_left.T, w_left_gate.T, w_right.T, w_right_gate.T,
+        w_gate_out, w_out, norm_in_gain[None], norm_out_gain[None],
     )
 
 

time: 53.8 us -> 40.3 us (0.75)
  local copies, waits for them, and re-layouts: 10 us -> 1.57 us
  other arithmetic: 2.92 us -> 0 us
  Pallas kernels: 39.5 us -> 37.8 us
    unnamed x5 -> x1, local copies, waits for them, and re-layouts: 4.89 us -> 1.57 us
    another operation x4 -> x0, local copies, waits for them, and re-layouts: 3.13 us -> none  [the longest x2 1.24 us: body(): gain_out = jnp.tile(norm_out_gain, 2)[None, :]]
    concatenate x2 -> x0, other arithmetic: 2.23 us -> none  [the longest x1 1.42 us: twice(): jnp.concatenate([jnp.concatenate([a, zero], 1), jnp.concatenate([zero, a]...]
    pallas_call x1, Pallas kernels: 39.5 us -> 37.8 us  [body(): pl.pallas_call(functools.partial(kernel, R, LN), out_shape=jax.ShapeDtype...]
    broadcast_in_dim x3 -> x0, local copies, waits for them, and re-layouts: 0.92 us -> none  [the longest x1 0.76 us: body(): col_valid = jnp.broadcast_to(col_valid[:, None], (cols, width))]
    reshape x2 -> x0, local copies, waits for them, and re-layouts: 0.77 us -> none  [body(): row_valid = jnp.repeat(row_valid.reshape(2, half).T, CH, axis=1)]
    convert_element_type x1 -> x0, other arithmetic: 0.68 us -> none  [body(): valid = token_mask.astype(F32)]
where the time goes in v2:
time: 40.3 us; the launch traced here: 40 us
  Pallas kernels  37.8 us (94%)
  local copies, waits for them, and re-layouts  1.57 us (4%)
  between operations  0.66 us (2%)
    pallas_call x1, Pallas kernels, body(): pl.pallas_call(functools.partial(kernel, R, LN), out_shape=jax.ShapeDtype...  37.8 us
    unnamed x1, local copies, waits for them, and re-layouts  1.57 us

profile of v2, /device:TPU:3, one launch (start us, length us, event | category | flops | bytes accessed | tf_op | source)
XLA Modules:
  0.0 40.0 jit_solution(12502137257566040829)
XLA Ops:
  0.7 37.8 %shard_map.109 = bf16[2,256,128]{2,1,0:T(8,128)(2,1)} custom-call(s32[1]{0:T(128)S(6)} %copy.13.start_ref, s32[1,512]{1,0:T(1,128)} %bitcast.11, bf16[64,256,128]{2,1,0:T(8,128)(2,1)} %pair_hbm.1, bf16[64,128]{1,0:T(8,128)(2,1)} %bitcast.7, bf16[64,128]{1,0:T(8,128)(2,1)} %bitcast.8, bf16[64,128]{1,0:T(8,128)(2,1)} %bitcast.9, bf16[64,128]{1,0:T(8,128)(2,1)} %bitcast.10, ...), custom_call_target="tpu_custom_call" | custom-call | tf_op jit(solution)/shard_map/pallas_call | solution.py:361
  38.5 1.6 %copy.14 = bf16[2,256,128]{2,1,0:T(8,128)(2,1)} copy(bf16[2,256,128]{2,1,0:T(8,128)(2,1)} %shard_map.109) | data formatting | bytes 262144

commit v3 on v2

--- a/solution.py
+++ b/solution.py
@@ -98,6 +98,25 @@
 
     lax.fori_loop(1, R * LN, greet, 0)
 
+    load.wait()
+
+    def candidate(t):
+        return pair[jnp.clip(start + t - me * rows_dev, 0, rows_dev - 1)]
+
+    def fill_a(i, _):
+        t = (i // 2) * 4 + (1 - core) * 2 + i % 2
+        send_a[i] = candidate(t)
+        return 0
+
+    lax.fori_loop(0, R, fill_a, 0)
+
+    pl.semaphore_wait(barrier, R * LN - 1)
+    copy_a = pltpu.make_async_remote_copy(
+        src_ref=send_a, dst_ref=recv_a, send_sem=a_sem.at[0], recv_sem=a_sem.at[1],
+        device_id=at(sib), device_id_type=MESH,
+    )
+    copy_a.start()
+
     def same_block(size, block):
         i = lax.broadcasted_iota(jnp.int32, (size, size), 0) // block
         j = lax.broadcasted_iota(jnp.int32, (size, size), 1) // block
@@ -139,24 +158,6 @@
     w_out2 = jnp.concatenate(
         [jnp.concatenate([w_out[...], zero_out], 1), jnp.concatenate([zero_out, w_out[...]], 1)], 0
     )
-    load.wait()
-
-    def candidate(t):
-        return pair[jnp.clip(start + t - me * rows_dev, 0, rows_dev - 1)]
-
-    def fill_a(i, _):
-        t = (i // 2) * 4 + (1 - core) * 2 + i % 2
-        send_a[i] = candidate(t)
-        return 0
-
-    lax.fori_loop(0, R, fill_a, 0)
-
-    pl.semaphore_wait(barrier, R * LN - 1)
-    copy_a = pltpu.make_async_remote_copy(
-        src_ref=send_a, dst_ref=recv_a, send_sem=a_sem.at[0], recv_sem=a_sem.at[1],
-        device_id=at(sib), device_id_type=MESH,
-    )
-    copy_a.start()
 
     def right_rows(jp):
         x = jnp.concatenate([pair[jp], pair[jp + half]], axis=1)
@@ -191,7 +192,7 @@
             device_id=at(peer * 2 + core), device_id_type=MESH,
         )
 
-    for i in range(1, Z):
+    for i in sorted(range(1, Z), key=lambda i: -abs(i - Z // 2)):
         copy_b(i).start()
     recv_b[z] = send_b[z]
     right_loop(half // 8, half)
@@ -205,12 +206,13 @@
     factor = sigmoid(both[:, width:]) * both[:, :width] * left_valid * col_valid[...]
     left_all[me] = factor.astype(BF16)
 
-    def copy_l(i):
-        peer = ((z + i) % Z) * 2 + core
+    def copy_l(i, peer=None):
+        if peer is None:
+            peer = sib if i == 0 else ((z + i) % Z) * 2 + core
         return pltpu.make_async_remote_copy(
             src_ref=left_all.at[me], dst_ref=left_all.at[me],
             send_sem=l_send_sem.at[i], recv_sem=l_recv_sem.at[i, 0],
-            device_id=at(sib if i == 0 else peer), device_id_type=MESH,
+            device_id=at(peer), device_id_type=MESH,
         )
 
     def forward(i):
@@ -221,7 +223,7 @@
             device_id=at(sib), device_id_type=MESH,
         )
 
-    for i in range(1, Z):
+    for i in sorted(range(1, Z), key=lambda i: -abs(i - Z // 2)):
         copy_l(i).start()
     copy_l(0).start()
     for i in range(2):
@@ -283,11 +285,15 @@
 
     copy_l(0).wait_recv()
     group_product(z)
-    for i in range(1, Z):
-        copy_l(i).wait_recv()
-        forward(i).start()
+    copy_l(1).wait_recv()
+    forward(1).start()
 
     def rest(i, _):
+        @pl.when(i < Z - 1)
+        def _():
+            copy_l(i + 1, sib).wait_recv()
+            forward(i + 1).start()
+
         forward(i).wait_recv()
         group_product((z + Z - i) % Z)
         return 0

time: 40.3 us -> 39.1 us (0.970)
  Pallas kernels: 37.8 us -> 36.5 us
    pallas_call x1, Pallas kernels: 37.8 us -> 36.5 us  [body(): pl.pallas_call(functools.partial(kernel, R, LN), out_shape=jax.ShapeDtype...]
where the time goes in v3:
time: 39.1 us; the launch traced here: 38.7 us
  Pallas kernels  36.5 us (93%)
  local copies, waits for them, and re-layouts  1.57 us (4%)
  between operations  0.66 us (2%)
    pallas_call x1, Pallas kernels, body(): pl.pallas_call(functools.partial(kernel, R, LN), out_shape=jax.ShapeDtype...  36.5 us
    unnamed x1, local copies, waits for them, and re-layouts  1.57 us

profile of v3, /device:TPU:3, one launch (start us, length us, event | category | flops | bytes accessed | tf_op | source)
XLA Modules:
  0.0 38.7 jit_solution(3792849060051826919)
XLA Ops:
  0.7 36.5 %shard_map.109 = bf16[2,256,128]{2,1,0:T(8,128)(2,1)} custom-call(s32[1]{0:T(128)S(6)} %copy.13.start_ref, s32[1,512]{1,0:T(1,128)} %bitcast.11, bf16[64,256,128]{2,1,0:T(8,128)(2,1)} %pair_hbm.1, bf16[64,128]{1,0:T(8,128)(2,1)} %bitcast.7, bf16[64,128]{1,0:T(8,128)(2,1)} %bitcast.8, bf16[64,128]{1,0:T(8,128)(2,1)} %bitcast.9, bf16[64,128]{1,0:T(8,128)(2,1)} %bitcast.10, ...), custom_call_target="tpu_custom_call" | custom-call | tf_op jit(solution)/shard_map/pallas_call | solution.py:367
  37.2 1.6 %copy.14 = bf16[2,256,128]{2,1,0:T(8,128)(2,1)} copy(bf16[2,256,128]{2,1,0:T(8,128)(2,1)} %shard_map.109) | data formatting | bytes 262144
